TPU v7x, 32 devices: a whole 2x2x4 slice. The times are simulated.
32 devices in a mesh: case: 2 (over y), blk: 4 (over z), split: 2 (over x), sub: 2 (over core).
Axes of the slice: x: 2, y: 2, z: 4, core: 2. Of those that a mesh axis runs over, the one named last changes fastest.
Arguments:
- cell_series: bfloat16 [32768, 4, 512], P(('case', 'blk', 'split', 'sub')), parts along dimension 0, may hold values from -6 to 6
- cell_count: int32 [32], P(('case', 'blk', 'split', 'sub')), parts along dimension 0, may hold values from 768 to 1024, as said below
- cell_target: int32 [32768], P(('case', 'blk', 'split', 'sub')), parts along dimension 0, may hold values from 0 to 2047, as said below
- surface: float32 [4, 8192], P(None, ('case', 'blk', 'split', 'sub')), parts along dimension 1, may hold values from -8.5 to 16.5, as said below
- observers: float32 [3, 1024], P(None, 'case'), parts along dimension 1, may hold values from -45 to 53, as said below
Outputs:
- pressure: float32 [1024, 2, 8], P(('case', 'blk')), parts along dimension 0
There are 2 independent parts, one for each index of `case`. A program takes and returns all parts, laid end to end along the dimension named above; each array names one. Nothing has to cross between parts.
Inputs may be any that keep to these rules, and one draw needn't show every extreme that they name: Cells i of a device with i < cell_count are live. `cell_target`: an entry t names local surface point t mod 256 of the device whose index along blk+split is t // 256 and whose sub index is the cell's. Among the rows of one device no such owner is named more than 192 times; in every device one owner is named by exactly 192 live rows, the same owner for all devices of one sub index. Every surface point lies within 8.5 of the point (8, 0, 0); panel areas are positive. `observers`: every observer lies 18 or more from the point (8, 0, 0).
All inputs are finite; a program needn't handle non-finite values.
Results may differ from a plain program's by a relative error of at most 0.0027.
Values may be sent and summed in bfloat16 or wider, within the bound.
A program may use at most 64 MiB of HBM per device.

v0:
```python
import math
import jax
import jax.numpy as jnp
from jax import lax
from jax.sharding import PartitionSpec as P

NF = 8


def spectral_lookup_matrix(signal_readings):
    clock_moments = jnp.arange(signal_readings, dtype=jnp.int32)
    spectral_slot_number = jnp.arange(NF, dtype=jnp.int32) + signal_readings // 16
    modulo_angle_value = spectral_slot_number[:, None] * clock_moments[None, :] % signal_readings
    phases = 2.0 * math.pi / signal_readings * modulo_angle_value.astype(jnp.float32)
    hann_attenuation_curve = 0.5 - 0.5 * jnp.cos(
        2.0 * math.pi / signal_readings * clock_moments.astype(jnp.float32)
    )
    scaled = 2.0 / signal_readings * hann_attenuation_curve[None, :]
    return jnp.concatenate([scaled * jnp.cos(phases), -scaled * jnp.sin(phases)], axis=0).astype(
        jnp.bfloat16
    )


def radiate(spectra, surface, listeners, amplitude):
    delta_x = listeners[0][:, None] - surface[0][None, :]
    delta_y = listeners[1][:, None] - surface[1][None, :]
    delta_z = listeners[2][:, None] - surface[2][None, :]
    radius = jnp.sqrt(delta_x * delta_x + delta_y * delta_y + delta_z * delta_z)
    inverse = 1.0 / radius
    normal_x = delta_x * inverse
    normal_y = delta_y * inverse
    normal_z = delta_z * inverse
    quadrature_factor = surface[3][None, :] * inverse * (amplitude / (4.0 * math.pi))
    blocks = spectra.reshape(2, NF, 4, spectra.shape[1])
    real_list = []
    imag_list = []
    for harmonic in range(NF):
        wavenumber = 0.5 + 0.25 * harmonic
        real_part = blocks[0, harmonic]
        imag_part = blocks[1, harmonic]
        load_real = (
            real_part[1][None, :] * normal_x
            + real_part[2][None, :] * normal_y
            + real_part[3][None, :] * normal_z
        )
        load_imag = (
            imag_part[1][None, :] * normal_x
            + imag_part[2][None, :] * normal_y
            + imag_part[3][None, :] * normal_z
        )
        source_real = (
            -wavenumber * imag_part[0][None, :] + load_real * inverse - wavenumber * load_imag
        )
        source_imag = (
            wavenumber * real_part[0][None, :] + wavenumber * load_real + load_imag * inverse
        )
        cosine = jnp.cos(wavenumber * radius)
        sinusoid = jnp.sin(wavenumber * radius)
        real_list.append(
            jnp.sum(quadrature_factor * (source_real * cosine + source_imag * sinusoid), axis=1)
        )
        imag_list.append(
            jnp.sum(quadrature_factor * (source_imag * cosine - source_real * sinusoid), axis=1)
        )
    real_out = jnp.stack(real_list, axis=1)
    imag_out = jnp.stack(imag_list, axis=1)
    return jnp.stack([real_out, imag_out], axis=1)


def local(cell_series, cell_count, cell_target, surface, observers):
    rows_dev = cell_series.shape[0]
    signal_readings = cell_series.shape[2]
    points_dev = surface.shape[1]
    source_groups = lax.axis_size("blk") * lax.axis_size("split")
    devices = source_groups * lax.axis_size("sub")
    capacity = (3 * rows_dev + 2 * source_groups - 1) // (2 * source_groups)
    slot_total = source_groups * capacity
    amplitude = 150.0 * math.sqrt(
        signal_readings * points_dev / (rows_dev * (points_dev * devices))
    )
    twiddle = spectral_lookup_matrix(signal_readings)
    row_index = jnp.arange(rows_dev, dtype=jnp.int32)
    active = row_index < cell_count[0]
    owner_index = cell_target // points_dev
    point_index = cell_target % points_dev
    matches = (
        (owner_index[:, None] == jnp.arange(source_groups, dtype=jnp.int32)[None, :])
        & active[:, None]
    ).astype(jnp.int32)
    sorted_ranking = jnp.sum(jnp.cumsum(matches, axis=0) * matches, axis=1) - 1
    destination = jnp.where(active, owner_index * capacity + sorted_ranking, slot_total)
    slot_source = (
        jnp.full((slot_total + 1,), rows_dev, jnp.int32).at[destination].set(row_index)[:slot_total]
    )
    slot_point = jnp.take(point_index, slot_source, mode="fill", fill_value=-1)
    flattened = cell_series.reshape(rows_dev * 4, signal_readings)
    per_cell = jnp.einsum("jt,rt->jr", twiddle, flattened, preferred_element_type=jnp.float32)
    per_cell = per_cell.reshape(2 * NF, rows_dev, 4).transpose(1, 0, 2).reshape(rows_dev, 8 * NF)
    outgoing = jnp.take(per_cell, slot_source, axis=0, mode="fill", fill_value=0.0)
    arrived_points, arrived = (
        lax.all_to_all(
            slot_point.reshape(source_groups, capacity),
            ("blk", "split"),
            split_axis=0,
            concat_axis=0,
            tiled=True,
        ),
        lax.all_to_all(
            outgoing.reshape(source_groups, capacity, 8 * NF),
            ("blk", "split"),
            split_axis=0,
            concat_axis=0,
            tiled=True,
        ),
    )
    arrived_points = arrived_points.reshape(slot_total)
    placing = (arrived_points[:, None] == jnp.arange(points_dev, dtype=jnp.int32)[None, :]).astype(
        jnp.float32
    )
    spectra = jnp.dot(
        arrived.reshape(slot_total, 8 * NF).T,
        placing,
        precision=lax.Precision.HIGHEST,
        preferred_element_type=jnp.float32,
    )
    summed = lax.psum_scatter(
        radiate(spectra, surface, observers, amplitude), "blk", scatter_dimension=0, tiled=True
    )
    return lax.psum(summed, ("split", "sub"))


def solution(mesh):
    return jax.shard_map(
        local,
        mesh=mesh,
        in_specs=(
            P(("case", "blk", "split", "sub"), None, None),
            P(("case", "blk", "split", "sub")),
            P(("case", "blk", "split", "sub")),
            P(None, ("case", "blk", "split", "sub")),
            P(None, "case"),
        ),
        out_specs=P(("case", "blk"), None, None),
        check_vma=False,
    )
```

profile of v0, /device:TPU:0, one launch (start us, length us, event | category | flops | bytes accessed | tf_op | source)
XLA Modules:
  0.0 115.6 jit_solution(8116364706808095267)
XLA Ops:
  6.5 0.7 add_select_fusion.1
  7.9 2.3 %reduce-window.6 = s32[8,8,128]{2,1,0:T(8,128)S(1)} reduce-window(s32[8,8,128]{2,1,0:T(8,128)S(1)} %fusion.62, s32[]{:T(128)} %constant.50.clone.1), window={size=1x1x128 pad=0_0x0_0x127_0}, to_apply=%region_0.1 | reduce-window | flops 1040384 | bytes 65540 | tf_op jit(solution)/shard_map/reduce-window
  10.8 4.3 %scatter_custom_fusion = s32[1537]{0:T(1024)S(1)} fusion(s32[1024]{0:T(1024)S(1)} %compare_select_fusion.3, s32[1024]{0:T(1024)S(1)} %iota.57, s32[]{:T(128)} %constant.46.clone.1), kind=kCustom, calls=%fused_computation.159 | custom fusion | bytes 6152 | tf_op jit(solution)/shard_map/scatter | solution.py:93
  15.1 5.9 %gather_fusion.1 = s32[1536]{0:T(1024)S(1)} fusion(s32[1024]{0:T(1024)S(1)} %get-tuple-element.94, s32[2048]{0:T(1024)S(1)} %pad_clamp_fusion), kind=kCustom, calls=%fused_computation.1 | custom fusion | bytes 18432 | tf_op jit(solution)/shard_map/jit(_take)/gather | solution.py:95
  21.1 0.6 and_select_fusion
  21.8 7.3 %all-to-all-start.1 = ((s32[8,1,192]{2,1,0:T(1,128)}), s32[8,1,192]{2,1,0:T(1,128)S(1)}, u32[]{:S(2)}, u32[]{:S(2)}) async-start(s32[8,1,192]{2,1,0:T(1,128)} %and_select_fusion), calls=%async_computation.1 | async-start | bytes 16384 | tf_op jit(solution)/shard_map/all_to_all | solution.py:101
  29.3 3.4 %fusion.5 = f32[1024,16,4]{0,1,2:T(8,128)S(1)} fusion(bf16[1024,4,512]{2,1,0:T(4,128)(2,1)} %param.5, bf16[8,512]{1,0:T(8,128)(2,1)S(1)} %get-tuple-element.97, bf16[8,512]{1,0:T(8,128)(2,1)S(1)} %get-tuple-element.96), kind=kOutput, calls=%fused_computation.8 | convolution fusion | flops 67141632 | bytes 4472832 | tf_op jit(solution)/shard_map/jt,rt->jr/dot_general | solution.py:97
  33.2 2.6 %gather_fusion = f32[1536,64]{1,0:T(8,128)S(1)} fusion(f32[1024,64]{1,0:T(8,128)S(1)} %copy.23, s32[2048]{0:T(1024)S(1)} %pad_clamp_fusion), kind=kCustom, calls=%fused_computation | custom fusion | bytes 792576 | tf_op jit(solution)/shard_map/jit(_take)/gather | solution.py:99
  35.8 0.3 copy.24
  36.2 0.8 broadcast_select_fusion
  37.0 6.0 %all-to-all-start = ((f32[8,192,64]{1,2,0:T(8,128)}), f32[8,192,64]{1,2,0:T(8,128)S(1)}, u32[]{:S(2)}, u32[]{:S(2)}) async-start(f32[8,192,64]{1,2,0:T(8,128)} %broadcast_select_fusion), calls=%async_computation | async-start | bytes 1048576 | tf_op jit(solution)/shard_map/all_to_all | solution.py:108
  43.2 13.8 %all-to-all-done = f32[8,192,64]{1,2,0:T(8,128)S(1)} async-done(((f32[8,192,64]{1,2,0:T(8,128)}), f32[8,192,64]{1,2,0:T(8,128)S(1)}, u32[]{:S(2)}, u32[]{:S(2)}) %all-to-all-start) | async-done | bytes 393248 | tf_op jit(solution)/shard_map/all_to_all | solution.py:108
  57.6 0.8 fusion.3
  58.5 3.3 %multiply_reduce_fusion.8 = (f32[512]{0:T(512)S(1)}, f32[512]{0:T(512)S(1)}) fusion(f32[256]{0:T(256)S(1)} %bitcast.252, f32[512]{0:T(512)S(1)} %bitcast.156, f32[256]{0:T(256)S(1)} %bitcast.260, f32[512]{0:T(512)S(1)} %bitcast.164, f32[256]{0:T(256)S(1)} %bitcast.244, f32[512]{0:T(512)S(1)} %bitcast.148, f32[256]{0:T(256)S(1)} %bitcast.229, ...), kind=kLoop, calls=%fused_computation.27 | loop fusion | flops 5635072 | bytes 22528 | tf_op jit(solution)/shard_map/reduce_sum | solution.py:60
  61.8 3.1 %multiply_reduce_fusion.9 = (f32[512]{0:T(512)S(1)}, f32[512]{0:T(512)S(1)}) fusion(f32[256]{0:T(256)S(1)} %bitcast.253, f32[512]{0:T(512)S(1)} %bitcast.157, f32[256]{0:T(256)S(1)} %bitcast.261, f32[512]{0:T(512)S(1)} %bitcast.165, f32[256]{0:T(256)S(1)} %bitcast.245, f32[512]{0:T(512)S(1)} %bitcast.149, f32[256]{0:T(256)S(1)} %bitcast.221, ...), kind=kLoop, calls=%fused_computation.32 | loop fusion | flops 5635072 | bytes 22528 | tf_op jit(solution)/shard_map/reduce_sum | solution.py:60
  64.9 3.1 %multiply_reduce_fusion.10 = (f32[512]{0:T(512)S(1)}, f32[512]{0:T(512)S(1)}) fusion(f32[256]{0:T(256)S(1)} %bitcast.254, f32[512]{0:T(512)S(1)} %bitcast.158, f32[256]{0:T(256)S(1)} %bitcast.262, f32[512]{0:T(512)S(1)} %bitcast.166, f32[256]{0:T(256)S(1)} %bitcast.246, f32[512]{0:T(512)S(1)} %bitcast.150, f32[256]{0:T(256)S(1)} %bitcast.213, ...), kind=kLoop, calls=%fused_computation.37 | loop fusion | flops 5635072 | bytes 22528 | tf_op jit(solution)/shard_map/reduce_sum | solution.py:60
  68.0 3.1 %multiply_reduce_fusion.11 = (f32[512]{0:T(512)S(1)}, f32[512]{0:T(512)S(1)}) fusion(f32[256]{0:T(256)S(1)} %bitcast.255, f32[512]{0:T(512)S(1)} %bitcast.159, f32[256]{0:T(256)S(1)} %bitcast.263, f32[512]{0:T(512)S(1)} %bitcast.167, f32[256]{0:T(256)S(1)} %bitcast.247, f32[512]{0:T(512)S(1)} %bitcast.151, f32[256]{0:T(256)S(1)} %bitcast.205, ...), kind=kLoop, calls=%fused_computation.82 | loop fusion | flops 5635072 | bytes 22528 | tf_op jit(solution)/shard_map/reduce_sum | solution.py:60
  71.1 3.1 %multiply_reduce_fusion.12 = (f32[512]{0:T(512)S(1)}, f32[512]{0:T(512)S(1)}) fusion(f32[256]{0:T(256)S(1)} %bitcast.256, f32[512]{0:T(512)S(1)} %bitcast.160, f32[256]{0:T(256)S(1)} %bitcast.264, f32[512]{0:T(512)S(1)} %bitcast.168, f32[256]{0:T(256)S(1)} %bitcast.248, f32[512]{0:T(512)S(1)} %bitcast.152, f32[256]{0:T(256)S(1)} %bitcast.197, ...), kind=kLoop, calls=%fused_computation.85 | loop fusion | flops 5635072 | bytes 22528 | tf_op jit(solution)/shard_map/reduce_sum | solution.py:60
  74.2 3.0 %multiply_reduce_fusion.13 = (f32[512]{0:T(512)S(1)}, f32[512]{0:T(512)S(1)}) fusion(f32[256]{0:T(256)S(1)} %bitcast.257, f32[512]{0:T(512)S(1)} %bitcast.161, f32[256]{0:T(256)S(1)} %bitcast.265, f32[512]{0:T(512)S(1)} %bitcast.169, f32[256]{0:T(256)S(1)} %bitcast.249, f32[512]{0:T(512)S(1)} %bitcast.153, f32[256]{0:T(256)S(1)} %bitcast.189, ...), kind=kLoop, calls=%fused_computation.88 | loop fusion | flops 5241856 | bytes 22528 | tf_op jit(solution)/shard_map/reduce_sum | solution.py:60
  77.2 3.1 %multiply_reduce_fusion.14 = (f32[512]{0:T(512)S(1)}, f32[512]{0:T(512)S(1)}) fusion(f32[256]{0:T(256)S(1)} %bitcast.258, f32[512]{0:T(512)S(1)} %bitcast.162, f32[256]{0:T(256)S(1)} %bitcast.266, f32[512]{0:T(512)S(1)} %bitcast.170, f32[256]{0:T(256)S(1)} %bitcast.250, f32[512]{0:T(512)S(1)} %bitcast.154, f32[256]{0:T(256)S(1)} %bitcast.181, ...), kind=kLoop, calls=%fused_computation.91 | loop fusion | flops 5635072 | bytes 22528 | tf_op jit(solution)/shard_map/reduce_sum | solution.py:60
  80.3 3.1 %multiply_reduce_fusion.15 = (f32[512]{0:T(512)S(1)}, f32[512]{0:T(512)S(1)}) fusion(f32[256]{0:T(256)S(1)} %bitcast.259, f32[512]{0:T(512)S(1)} %bitcast.163, f32[256]{0:T(256)S(1)} %bitcast.267, f32[512]{0:T(512)S(1)} %bitcast.171, f32[256]{0:T(256)S(1)} %bitcast.251, f32[512]{0:T(512)S(1)} %bitcast.155, f32[256]{0:T(256)S(1)} %bitcast.173, ...), kind=kLoop, calls=%fused_computation.94 | loop fusion | flops 5635072 | bytes 22528 | tf_op jit(solution)/shard_map/reduce_sum | solution.py:60
  83.5 0.6 pad_maximum_fusion
  84.1 18.1 %reduce-scatter.2.cloned.1.call-done = f32[128,2,8]{0,2,1:T(8,128)} async-done(((f32[512,2,8]{0,2,1:T(8,128)}), f32[128,2,8]{0,2,1:T(8,128)}) %reduce-scatter.2.cloned.1.call-update) | async-done | bytes 8208 | tf_op jit(solution)/shard_map/reduce_scatter | solution.py:126
  102.3 6.4 %psum.7 = f32[128,2,8]{0,2,1:T(8,128)} all-reduce(f32[128,2,8]{0,2,1:T(8,128)} %reduce-scatter.2.cloned.1.call-done), channel_id=1, replica_groups=mesh['case'=2,'blk'=4,'split'=2,'sub'=2] {'split','sub'}, use_global_device_ids=true, to_apply=%region_21.22 | all-reduce | flops 2048 | bytes 16384 | tf_op jit(solution)/shard_map/psum | solution.py:129
  (41 shorter events, 2.4 us)
Async XLA Ops:
  21.8 15.2 %all-to-all-start.1 = ((s32[8,1,192]{2,1,0:T(1,128)}), s32[8,1,192]{2,1,0:T(1,128)S(1)}, u32[]{:S(2)}, u32[]{:S(2)}) async-start(s32[8,1,192]{2,1,0:T(1,128)} %and_select_fusion), calls=%async_computation.1 | async-start | bytes 16384 | tf_op jit(solution)/shard_map/all_to_all | solution.py:101
  33.2 9.9 %copy-start.1 = (f32[4,256]{1,0:T(4,128)S(1)}, f32[4,256]{1,0:T(4,128)}, u32[]{:S(2)}) copy-start(f32[4,256]{1,0:T(4,128)} %param.8) | copy-start | bytes 12292
  33.2 9.9 %copy-start = (f32[3,512]{1,0:T(4,128)S(1)}, f32[3,512]{1,0:T(4,128)}, u32[]{:S(2)}) copy-start(f32[3,512]{1,0:T(4,128)} %param.9) | copy-start | bytes 18436
  37.0 20.0 %all-to-all-start = ((f32[8,192,64]{1,2,0:T(8,128)}), f32[8,192,64]{1,2,0:T(8,128)S(1)}, u32[]{:S(2)}, u32[]{:S(2)}) async-start(f32[8,192,64]{1,2,0:T(8,128)} %broadcast_select_fusion), calls=%async_computation | async-start | bytes 1048576 | tf_op jit(solution)/shard_map/all_to_all | solution.py:108
  43.0 59.3 %reduce-scatter.2.cloned.1.call-start = ((), (), s32[]{:S(2)}) async-start(), calls=%async_computation.3 | async-start | bytes 40960 | tf_op jit(solution)/shard_map/reduce_scatter | solution.py:126
Sparse Core Ops, SparseCore 0:
  84.3 17.9 reduce-scatter.1
where the time goes:
time: 116 us
  waiting for transfers between devices  31.9 us (28%)
  other arithmetic  30.6 us (26%)
  local copies, waits for them, and re-layouts  14.8 us (13%)
  between operations  14.3 us (12%)
  starting transfers between devices  13.3 us (11%)
  blocking collectives  6.44 us (6%)
  matrix products  4.22 us (4%)
    reduce_sum x8, other arithmetic, radiate(): jnp.sum(quadrature_factor * (source_real * cosine + source_imag * sinusoi...  24.9 us
    reduce_scatter x1, waiting for transfers between devices, local(): lax.psum_scatter(radiate(spectra, surface, observers, amplitude), 'blk',...  18.1 us
    all_to_all x1, waiting for transfers between devices, local(): lax.all_to_all(outgoing.reshape(source_groups, capacity, 8 * NF), ('blk',...  13.8 us
    all_to_all x1, starting transfers between devices, local(): lax.all_to_all(slot_point.reshape(source_groups, capacity), ('blk', 'spli...  7.25 us
    psum x1, blocking collectives, local(): return lax.psum(summed, ('split', 'sub'))  6.44 us
    all_to_all x1, starting transfers between devices, local(): lax.all_to_all(outgoing.reshape(source_groups, capacity, 8 * NF), ('blk',...  6 us
    gather x2, local copies, waits for them, and re-layouts, local(): slot_point = jnp.take(point_index, slot_source, mode='fill', fill_value=-1)  5.93 us
    scatter x1, local copies, waits for them, and re-layouts, local(): jnp.full((slot_total + 1,), rows_dev, jnp.int32).at[destination]  4.32 us
  transfers between devices with their start and end apart: 3, of which 2 were waited for; matrix products, arithmetic and copies ran while one was open for 7% of the time, Pallas kernels for 0%

commit v1 on v0

--- a/solution.py
+++ b/solution.py
@@ -126,7 +126,7 @@
     summed = lax.psum_scatter(
         radiate(spectra, surface, observers, amplitude), "blk", scatter_dimension=0, tiled=True
     )
-    return lax.psum(summed, ("split", "sub"))
+    return lax.psum(lax.psum(summed, "sub"), "split")
 
 
 def solution(mesh):

time: 116 us -> 118 us (1.017)
  blocking collectives: 6.44 us -> 8.16 us
    psum x1 -> x2, blocking collectives: 6.44 us -> 8.16 us  [local(): return lax.psum(lax.psum(summed, 'sub'), 'split')]
where the time goes in v1:
time: 118 us; the launch traced here: 117 us
  waiting for transfers between devices  31.9 us (27%)
  other arithmetic  30.6 us (26%)
  local copies, waits for them, and re-layouts  14.8 us (13%)
  between operations  14.3 us (12%)
  starting transfers between devices  13.3 us (11%)
  blocking collectives  8.16 us (7%)
  matrix products  4.22 us (4%)
    reduce_sum x8, other arithmetic, radiate(): jnp.sum(quadrature_factor * (source_real * cosine + source_imag * sinusoi...  24.9 us
    reduce_scatter x1, waiting for transfers between devices, local(): lax.psum_scatter(radiate(spectra, surface, observers, amplitude), 'blk',...  18.1 us
    all_to_all x1, waiting for transfers between devices, local(): lax.all_to_all(outgoing.reshape(source_groups, capacity, 8 * NF), ('blk',...  13.8 us
    psum x2, blocking collectives, local(): return lax.psum(lax.psum(summed, 'sub'), 'split')  8.16 us
    all_to_all x1, starting transfers between devices, local(): lax.all_to_all(slot_point.reshape(source_groups, capacity), ('blk', 'spli...  7.25 us
    all_to_all x1, starting transfers between devices, local(): lax.all_to_all(outgoing.reshape(source_groups, capacity, 8 * NF), ('blk',...  6 us
    gather x2, local copies, waits for them, and re-layouts, local(): slot_point = jnp.take(point_index, slot_source, mode='fill', fill_value=-1)  5.93 us
    scatter x1, local copies, waits for them, and re-layouts, local(): jnp.full((slot_total + 1,), rows_dev, jnp.int32).at[destination]  4.32 us
  transfers between devices with their start and end apart: 3, of which 2 were waited for; matrix products, arithmetic and copies ran while one was open for 7% of the time, Pallas kernels for 0%

profile of v1, /device:TPU:0, one launch (start us, length us, event | category | flops | bytes accessed | tf_op | source)
XLA Modules:
  0.0 117.3 jit_solution(10347456890335686757)
XLA Ops:
  6.5 0.7 add_select_fusion.1
  7.9 2.3 %reduce-window.6 = s32[8,8,128]{2,1,0:T(8,128)S(1)} reduce-window(s32[8,8,128]{2,1,0:T(8,128)S(1)} %fusion.62, s32[]{:T(128)} %constant.50.clone.1), window={size=1x1x128 pad=0_0x0_0x127_0}, to_apply=%region_0.1 | reduce-window | flops 1040384 | bytes 65540 | tf_op jit(solution)/shard_map/reduce-window
  10.8 4.3 %scatter_custom_fusion = s32[1537]{0:T(1024)S(1)} fusion(s32[1024]{0:T(1024)S(1)} %compare_select_fusion.3, s32[1024]{0:T(1024)S(1)} %iota.57, s32[]{:T(128)} %constant.46.clone.1), kind=kCustom, calls=%fused_computation.159 | custom fusion | bytes 6152 | tf_op jit(solution)/shard_map/scatter | solution.py:93
  15.1 5.9 %gather_fusion.1 = s32[1536]{0:T(1024)S(1)} fusion(s32[1024]{0:T(1024)S(1)} %get-tuple-element.94, s32[2048]{0:T(1024)S(1)} %pad_clamp_fusion), kind=kCustom, calls=%fused_computation.1 | custom fusion | bytes 18432 | tf_op jit(solution)/shard_map/jit(_take)/gather | solution.py:95
  21.1 0.6 and_select_fusion
  21.8 7.3 %all-to-all-start.1 = ((s32[8,1,192]{2,1,0:T(1,128)}), s32[8,1,192]{2,1,0:T(1,128)S(1)}, u32[]{:S(2)}, u32[]{:S(2)}) async-start(s32[8,1,192]{2,1,0:T(1,128)} %and_select_fusion), calls=%async_computation.1 | async-start | bytes 16384 | tf_op jit(solution)/shard_map/all_to_all | solution.py:101
  29.3 3.4 %fusion.5 = f32[1024,16,4]{0,1,2:T(8,128)S(1)} fusion(bf16[1024,4,512]{2,1,0:T(4,128)(2,1)} %param.5, bf16[8,512]{1,0:T(8,128)(2,1)S(1)} %get-tuple-element.97, bf16[8,512]{1,0:T(8,128)(2,1)S(1)} %get-tuple-element.96), kind=kOutput, calls=%fused_computation.8 | convolution fusion | flops 67141632 | bytes 4472832 | tf_op jit(solution)/shard_map/jt,rt->jr/dot_general | solution.py:97
  33.2 2.6 %gather_fusion = f32[1536,64]{1,0:T(8,128)S(1)} fusion(f32[1024,64]{1,0:T(8,128)S(1)} %copy.23, s32[2048]{0:T(1024)S(1)} %pad_clamp_fusion), kind=kCustom, calls=%fused_computation | custom fusion | bytes 792576 | tf_op jit(solution)/shard_map/jit(_take)/gather | solution.py:99
  36.2 0.8 broadcast_select_fusion
  37.0 6.0 %all-to-all-start = ((f32[8,192,64]{1,2,0:T(8,128)}), f32[8,192,64]{1,2,0:T(8,128)S(1)}, u32[]{:S(2)}, u32[]{:S(2)}) async-start(f32[8,192,64]{1,2,0:T(8,128)} %broadcast_select_fusion), calls=%async_computation | async-start | bytes 1048576 | tf_op jit(solution)/shard_map/all_to_all | solution.py:108
  43.2 13.8 %all-to-all-done = f32[8,192,64]{1,2,0:T(8,128)S(1)} async-done(((f32[8,192,64]{1,2,0:T(8,128)}), f32[8,192,64]{1,2,0:T(8,128)S(1)}, u32[]{:S(2)}, u32[]{:S(2)}) %all-to-all-start) | async-done | bytes 393248 | tf_op jit(solution)/shard_map/all_to_all | solution.py:108
  57.6 0.8 fusion.3
  58.5 3.3 %multiply_reduce_fusion.8 = (f32[512]{0:T(512)S(1)}, f32[512]{0:T(512)S(1)}) fusion(f32[256]{0:T(256)S(1)} %bitcast.252, f32[512]{0:T(512)S(1)} %bitcast.156, f32[256]{0:T(256)S(1)} %bitcast.260, f32[512]{0:T(512)S(1)} %bitcast.164, f32[256]{0:T(256)S(1)} %bitcast.244, f32[512]{0:T(512)S(1)} %bitcast.148, f32[256]{0:T(256)S(1)} %bitcast.229, ...), kind=kLoop, calls=%fused_computation.27 | loop fusion | flops 5635072 | bytes 22528 | tf_op jit(solution)/shard_map/reduce_sum | solution.py:60
  61.8 3.1 %multiply_reduce_fusion.9 = (f32[512]{0:T(512)S(1)}, f32[512]{0:T(512)S(1)}) fusion(f32[256]{0:T(256)S(1)} %bitcast.253, f32[512]{0:T(512)S(1)} %bitcast.157, f32[256]{0:T(256)S(1)} %bitcast.261, f32[512]{0:T(512)S(1)} %bitcast.165, f32[256]{0:T(256)S(1)} %bitcast.245, f32[512]{0:T(512)S(1)} %bitcast.149, f32[256]{0:T(256)S(1)} %bitcast.221, ...), kind=kLoop, calls=%fused_computation.32 | loop fusion | flops 5635072 | bytes 22528 | tf_op jit(solution)/shard_map/reduce_sum | solution.py:60
  64.9 3.1 %multiply_reduce_fusion.10 = (f32[512]{0:T(512)S(1)}, f32[512]{0:T(512)S(1)}) fusion(f32[256]{0:T(256)S(1)} %bitcast.254, f32[512]{0:T(512)S(1)} %bitcast.158, f32[256]{0:T(256)S(1)} %bitcast.262, f32[512]{0:T(512)S(1)} %bitcast.166, f32[256]{0:T(256)S(1)} %bitcast.246, f32[512]{0:T(512)S(1)} %bitcast.150, f32[256]{0:T(256)S(1)} %bitcast.213, ...), kind=kLoop, calls=%fused_computation.37 | loop fusion | flops 5635072 | bytes 22528 | tf_op jit(solution)/shard_map/reduce_sum | solution.py:60
  68.0 3.1 %multiply_reduce_fusion.11 = (f32[512]{0:T(512)S(1)}, f32[512]{0:T(512)S(1)}) fusion(f32[256]{0:T(256)S(1)} %bitcast.255, f32[512]{0:T(512)S(1)} %bitcast.159, f32[256]{0:T(256)S(1)} %bitcast.263, f32[512]{0:T(512)S(1)} %bitcast.167, f32[256]{0:T(256)S(1)} %bitcast.247, f32[512]{0:T(512)S(1)} %bitcast.151, f32[256]{0:T(256)S(1)} %bitcast.205, ...), kind=kLoop, calls=%fused_computation.82 | loop fusion | flops 5635072 | bytes 22528 | tf_op jit(solution)/shard_map/reduce_sum | solution.py:60
  71.1 3.1 %multiply_reduce_fusion.12 = (f32[512]{0:T(512)S(1)}, f32[512]{0:T(512)S(1)}) fusion(f32[256]{0:T(256)S(1)} %bitcast.256, f32[512]{0:T(512)S(1)} %bitcast.160, f32[256]{0:T(256)S(1)} %bitcast.264, f32[512]{0:T(512)S(1)} %bitcast.168, f32[256]{0:T(256)S(1)} %bitcast.248, f32[512]{0:T(512)S(1)} %bitcast.152, f32[256]{0:T(256)S(1)} %bitcast.197, ...), kind=kLoop, calls=%fused_computation.85 | loop fusion | flops 5635072 | bytes 22528 | tf_op jit(solution)/shard_map/reduce_sum | solution.py:60
  74.2 3.0 %multiply_reduce_fusion.13 = (f32[512]{0:T(512)S(1)}, f32[512]{0:T(512)S(1)}) fusion(f32[256]{0:T(256)S(1)} %bitcast.257, f32[512]{0:T(512)S(1)} %bitcast.161, f32[256]{0:T(256)S(1)} %bitcast.265, f32[512]{0:T(512)S(1)} %bitcast.169, f32[256]{0:T(256)S(1)} %bitcast.249, f32[512]{0:T(512)S(1)} %bitcast.153, f32[256]{0:T(256)S(1)} %bitcast.189, ...), kind=kLoop, calls=%fused_computation.88 | loop fusion | flops 5241856 | bytes 22528 | tf_op jit(solution)/shard_map/reduce_sum | solution.py:60
  77.2 3.1 %multiply_reduce_fusion.14 = (f32[512]{0:T(512)S(1)}, f32[512]{0:T(512)S(1)}) fusion(f32[256]{0:T(256)S(1)} %bitcast.258, f32[512]{0:T(512)S(1)} %bitcast.162, f32[256]{0:T(256)S(1)} %bitcast.266, f32[512]{0:T(512)S(1)} %bitcast.170, f32[256]{0:T(256)S(1)} %bitcast.250, f32[512]{0:T(512)S(1)} %bitcast.154, f32[256]{0:T(256)S(1)} %bitcast.181, ...), kind=kLoop, calls=%fused_computation.91 | loop fusion | flops 5635072 | bytes 22528 | tf_op jit(solution)/shard_map/reduce_sum | solution.py:60
  80.3 3.1 %multiply_reduce_fusion.15 = (f32[512]{0:T(512)S(1)}, f32[512]{0:T(512)S(1)}) fusion(f32[256]{0:T(256)S(1)} %bitcast.259, f32[512]{0:T(512)S(1)} %bitcast.163, f32[256]{0:T(256)S(1)} %bitcast.267, f32[512]{0:T(512)S(1)} %bitcast.171, f32[256]{0:T(256)S(1)} %bitcast.251, f32[512]{0:T(512)S(1)} %bitcast.155, f32[256]{0:T(256)S(1)} %bitcast.173, ...), kind=kLoop, calls=%fused_computation.94 | loop fusion | flops 5635072 | bytes 22528 | tf_op jit(solution)/shard_map/reduce_sum | solution.py:60
  83.5 0.6 pad_maximum_fusion
  84.1 18.1 %reduce-scatter.2.cloned.1.call-done = f32[128,2,8]{0,2,1:T(8,128)} async-done(((f32[512,2,8]{0,2,1:T(8,128)}), f32[128,2,8]{0,2,1:T(8,128)}) %reduce-scatter.2.cloned.1.call-update) | async-done | bytes 8208 | tf_op jit(solution)/shard_map/reduce_scatter | solution.py:126
  102.3 2.6 %psum.14 = f32[128,2,8]{0,2,1:T(8,128)S(1)} all-reduce(f32[128,2,8]{0,2,1:T(8,128)} %reduce-scatter.2.cloned.1.call-done), channel_id=1, replica_groups=mesh['case'=2,'blk'=4,'split'=2,'sub'=2] {'sub'}, use_global_device_ids=true, to_apply=%region_21.22 | all-reduce | flops 2048 | bytes 16384 | tf_op jit(solution)/shard_map/psum | solution.py:129
  104.9 5.6 %psum.15 = f32[128,2,8]{0,2,1:T(8,128)} all-reduce(f32[128,2,8]{0,2,1:T(8,128)S(1)} %psum.14), channel_id=1, replica_groups=mesh['case'=2,'blk'=4,'split'=2,'sub'=2] {'split'}, use_global_device_ids=true, to_apply=%region_22.23 | all-reduce | flops 2048 | bytes 16384 | tf_op jit(solution)/shard_map/psum | solution.py:129
  (42 shorter events, 2.7 us)
Async XLA Ops:
  21.8 15.2 %all-to-all-start.1 = ((s32[8,1,192]{2,1,0:T(1,128)}), s32[8,1,192]{2,1,0:T(1,128)S(1)}, u32[]{:S(2)}, u32[]{:S(2)}) async-start(s32[8,1,192]{2,1,0:T(1,128)} %and_select_fusion), calls=%async_computation.1 | async-start | bytes 16384 | tf_op jit(solution)/shard_map/all_to_all | solution.py:101
  33.2 9.9 %copy-start.1 = (f32[4,256]{1,0:T(4,128)S(1)}, f32[4,256]{1,0:T(4,128)}, u32[]{:S(2)}) copy-start(f32[4,256]{1,0:T(4,128)} %param.8) | copy-start | bytes 12292
  33.2 9.9 %copy-start = (f32[3,512]{1,0:T(4,128)S(1)}, f32[3,512]{1,0:T(4,128)}, u32[]{:S(2)}) copy-start(f32[3,512]{1,0:T(4,128)} %param.9) | copy-start | bytes 18436
  37.0 20.0 %all-to-all-start = ((f32[8,192,64]{1,2,0:T(8,128)}), f32[8,192,64]{1,2,0:T(8,128)S(1)}, u32[]{:S(2)}, u32[]{:S(2)}) async-start(f32[8,192,64]{1,2,0:T(8,128)} %broadcast_select_fusion), calls=%async_computation | async-start | bytes 1048576 | tf_op jit(solution)/shard_map/all_to_all | solution.py:108
  43.0 59.3 %reduce-scatter.2.cloned.1.call-start = ((), (), s32[]{:S(2)}) async-start(), calls=%async_computation.3 | async-start | bytes 40960 | tf_op jit(solution)/shard_map/reduce_scatter | solution.py:126
Sparse Core Ops, SparseCore 0:
  84.3 17.9 reduce-scatter.1
